TPU v7x, 32 devices: a whole 2x2x4 slice. The times are simulated.
32 devices in a mesh: tile: 8 (over y, x, core), lag: 4 (over z).
Axes of the slice: x: 2, y: 2, z: 4, core: 2. Of those that a mesh axis runs over, the one named last changes fastest.
Arguments:
- history: bfloat16 [8, 64, 384, 512], P('lag', 'tile'), may hold values from -6 to 6
- lag_blocks: bfloat16 [8, 64, 2, 384, 384], P('lag', 'tile'), may hold values from -0.09375 to 0.09375
- self_inverse: bfloat16 [64, 384, 384], P('tile'), may hold values from -0.3125 to 0.3125
- excitation: float32 [64, 384, 512], P('tile'), may hold values from -6 to 6
- pattern: int32 [8, 64, 2], P('lag', 'tile'), may hold values from 0 to 8
- live_counts: int32 [8, 64], P('lag', 'tile'), may hold values from 1 to 2
Outputs:
- traction: bfloat16 [64, 384, 512], P('tile')
- shifted_history: bfloat16 [8, 64, 384, 512], P('lag', 'tile')
All inputs are finite; a program needn't handle non-finite values.
Results may differ from a plain program's by a relative error of at most 0.013.
Values may be sent and summed in bfloat16 or wider, within the bound.
A program may use at most 128 MiB of HBM per device.

v0:
```python
import jax
import jax.numpy as jnp
from jax import lax
from jax.sharding import PartitionSpec as P

SLOTS = 2
EDGE = 4


def padded(cells, sides, width):
    for axis, dim in sides:
        count = lax.axis_size(axis)
        head = lax.slice_in_dim(cells, 0, width, axis=dim)
        tail = lax.slice_in_dim(cells, cells.shape[dim] - width, cells.shape[dim], axis=dim)
        cells = jnp.concatenate(
            [
                lax.ppermute(tail, axis, [(i, (i + 1) % count) for i in range(count)]),
                cells,
                lax.ppermute(head, axis, [((i + 1) % count, i) for i in range(count)]),
            ],
            axis=dim,
        )
    return cells


def passed_along(array, axis, by):
    length = lax.axis_size(axis)
    pairs = [(i, i + by) for i in range(length) if 0 <= i + by < length]
    return lax.ppermute(array, axis, pairs)


def pick_sources(window, source_index):
    return window[source_index]


def shards(history, lag_blocks, self_inverse, excitation, pattern, live_counts):
    blocks_here = history.shape[1]
    window = padded(history, (("tile", 1),), EDGE)
    positions = jnp.arange(blocks_here, dtype=jnp.int32)
    source_index = positions[None, :, None] + pattern
    sources = jax.vmap(pick_sources)(window, source_index)
    live = jnp.arange(SLOTS, dtype=jnp.int32)[None, None, :] < live_counts[:, :, None]
    sources = sources * live[:, :, :, None, None].astype(sources.dtype)
    partial_field = jnp.einsum(
        "lbsij,lbsjr->bir", lag_blocks, sources, preferred_element_type=jnp.float32
    )
    carried = passed_along(history[-1], "lag", 1)
    field = lax.psum(partial_field.astype(jnp.bfloat16), "lag").astype(jnp.float32)
    residual = (excitation - field).astype(jnp.bfloat16)
    traction = jnp.einsum(
        "bij,bjr->bir", self_inverse, residual, preferred_element_type=jnp.float32
    ).astype(jnp.bfloat16)
    newest = jnp.where(lax.axis_index("lag") == 0, traction, carried)
    shifted_history = jnp.concatenate([newest[None], history[:-1]], axis=0)
    return (traction, shifted_history)


def solution(mesh):
    in_specs = (
        P("lag", "tile", None, None),
        P("lag", "tile", None, None, None),
        P("tile", None, None),
        P("tile", None, None),
        P("lag", "tile", None),
        P("lag", "tile"),
    )
    out_specs = (P("tile", None, None), P("lag", "tile", None, None))
    return jax.shard_map(shards, mesh=mesh, in_specs=in_specs, out_specs=out_specs, check_vma=False)
```

profile of v0, /device:TPU:0, one launch (start us, length us, event | category | flops | bytes accessed | tf_op | source)
XLA Modules:
  0.0 329.3 jit_solution(16674762789030286297)
XLA Ops:
  7.2 0.0 copy-start
  7.2 0.0 copy-start.2
  7.2 0.0 copy-start.3
  7.2 0.0 all-reduce.2.cloned.1.call-start
  7.2 6.2 %fusion.13 = (bf16[2,4,384,512]{3,2,1,0:T(8,128)(2,1)}, bf16[2,4,384,512]{3,2,1,0:T(8,128)(2,1)}) fusion(bf16[2,8,384,512]{3,2,1,0:T(8,128)(2,1)} %param.6), kind=kLoop, calls=%fused_computation.20 | loop fusion | bytes 12582912 | tf_op jit(solution)/shard_map/slice | solution.py:14
  13.5 0.5 collective-permute-start
  13.9 2.9 collective-permute-start.1
  16.8 0.0 copy-done.2
  16.8 0.1 copy.14
  16.9 0.1 reshape.10
  17.0 0.0 copy-done.3
  17.0 0.1 fusion.7
  17.1 66.0 %collective-permute-done = bf16[2,4,384,512]{3,2,1,0:T(8,128)(2,1)} collective-permute-done((bf16[2,4,384,512]{3,2,1,0:T(8,128)(2,1)}, bf16[2,4,384,512]{3,2,1,0:T(8,128)(2,1)}, u32[]{:S(2)}, u32[]{:S(2)}) %collective-permute-start) | collective-permute-done | bytes 3145760 | tf_op jit(solution)/shard_map/ppermute | solution.py:17
  83.1 1.5 collective-permute-done.1
  84.7 10.5 %pad_maximum_fusion = bf16[2,16,384,512]{3,2,1,0:T(8,128)(2,1)} fusion(bf16[2,4,384,512]{3,2,1,0:T(8,128)(2,1)} %collective-permute-done.1, bf16[2,8,384,512]{3,2,1,0:T(8,128)(2,1)} %param.6, bf16[2,4,384,512]{3,2,1,0:T(8,128)(2,1)} %collective-permute-done), kind=kLoop, calls=%fused_computation.1 | loop fusion | flops 12582912 | bytes 25165824 | tf_op jit(solution)/shard_map/concatenate | solution.py:15
  95.2 11.4 %gather_fusion = bf16[32,384,512]{2,1,0:T(8,128)(2,1)} fusion(bf16[2,16,384,512]{3,2,1,0:T(8,128)(2,1)} %pad_maximum_fusion, s32[32]{0:T(128)S(1)} %reshape.10), kind=kCustom, calls=%fused_computation | custom fusion | bytes 25166080 | tf_op jit(solution)/shard_map/vmap()/gather | solution.py:33
  106.6 12.6 %fusion.4 = bf16[8,384,512]{2,1,0:T(8,128)(2,1)} fusion(bf16[2,8,2,384,384]{4,3,2,1,0:T(8,128)(2,1)} %param.7, bf16[2,8,2,384,512]{4,3,2,1,0:T(8,128)(2,1)} %bitcast.24, bf16[2,8,2]{2,1,0:T(8,128)(2,1)S(1)} %fusion.7), kind=kOutput, calls=%fused_computation.9 | convolution fusion | flops 4858576896 | bytes 25165888 | tf_op jit(solution)/shard_map/lbsij,lbsjr->bir/dot_general | solution.py:44
  119.2 0.0 all-reduce.2.cloned.1.call-update
  119.2 6.1 %fusion.12 = (bf16[1,8,384,512]{3,2,1,0:T(8,128)(2,1)}, bf16[1,8,384,512]{3,2,1,0:T(8,128)(2,1)}) fusion(bf16[2,8,384,512]{3,2,1,0:T(8,128)(2,1)} %param.6), kind=kLoop, calls=%fused_computation.19 | loop fusion | bytes 12582912 | tf_op jit(solution)/shard_map/slice | solution.py:47
  125.3 4.8 %copy.22 = bf16[1,8,384,512]{2,3,1,0:T(8,128)(2,1)} copy(bf16[1,8,384,512]{3,2,1,0:T(8,128)(2,1)} %get-tuple-element.6) | data formatting | bytes 6291456
  130.1 5.1 %collective-permute-start.2 = (bf16[8,384,512]{1,2,0:T(8,128)(2,1)}, bf16[8,384,512]{1,2,0:T(8,128)(2,1)}, u32[]{:S(2)}, u32[]{:S(2)}) collective-permute-start(bf16[8,384,512]{1,2,0:T(8,128)(2,1)} %bitcast.25), channel_id=1, source_target_pairs={{0,1},{1,2},{2,3},{4,5},{5,6},{6,7},{8,9},{9,10},{10,11},{12,13},{... | collective-permute-start | bytes 9437192 | tf_op jit(solution)/shard_map/ppermute | solution.py:29
  135.2 4.7 %copy.23 = bf16[1,8,384,512]{2,3,1,0:T(8,128)(2,1)} copy(bf16[1,8,384,512]{3,2,1,0:T(8,128)(2,1)} %get-tuple-element.7) | data formatting | bytes 6291456
  139.8 155.6 %all-reduce.2.cloned.1.call-done = bf16[8,384,512]{2,1,0:T(8,128)(2,1)} async-done(((bf16[8,384,512]{2,1,0:T(8,128)(2,1)}), bf16[8,384,512]{2,1,0:T(8,128)(2,1)}) %all-reduce.2.cloned.1.call-update) | async-done | bytes 3145744 | tf_op jit(solution)/shard_map/psum | solution.py:48
  295.4 0.0 copy-done
  295.4 7.6 %convert_bitcast_fusion = bf16[8,384,512]{1,2,0:T(8,128)(2,1)} fusion(bf16[8,384,384]{2,1,0:T(8,128)(2,1)S(1)} %copy-done, f32[8,384,512]{2,1,0:T(8,128)} %param.9, bf16[8,384,512]{2,1,0:T(8,128)(2,1)} %all-reduce.2.cloned.1.call-done), kind=kOutput, calls=%fused_computation.11 | convolution fusion | flops 1214251008 | bytes 14942208 | tf_op jit(solution)/shard_map/bij,bjr->bir/dot_general | solution.py:50
  303.0 4.6 %copy.18 = bf16[8,384,512]{2,1,0:T(8,128)(2,1)} copy(bf16[8,384,512]{1,2,0:T(8,128)(2,1)} %convert_bitcast_fusion) | data formatting | bytes 6291456
  307.6 0.0 copy-start.1
  307.7 0.0 collective-permute-done.2
  307.7 2.4 select_bitcast_fusion
  310.1 0.4 copy-done.1
  310.5 3.4 %pad_maximum_fusion.1 = bf16[2,8,384,512]{2,3,1,0:T(8,128)(2,1)} fusion(bf16[1,8,384,512]{2,3,1,0:T(8,128)(2,1)S(1)} %copy-done.1, bf16[1,8,384,512]{2,3,1,0:T(8,128)(2,1)S(1)} %select_bitcast_fusion), kind=kLoop, calls=%fused_computation.4 | loop fusion | flops 3145728 | bytes 12582912 | tf_op jit(solution)/shard_map/concatenate | solution.py:54
  313.8 8.6 %copy.19 = bf16[2,8,384,512]{3,2,1,0:T(8,128)(2,1)} copy(bf16[2,8,384,512]{2,3,1,0:T(8,128)(2,1)} %pad_maximum_fusion.1) | data formatting | bytes 12582912
  (1 shorter events, 0.0 us)
Async XLA Ops:
  7.2 288.2 %copy-start = (bf16[8,384,384]{2,1,0:T(8,128)(2,1)S(1)}, bf16[8,384,384]{2,1,0:T(8,128)(2,1)}, u32[]{:S(2)}) copy-start(bf16[8,384,384]{2,1,0:T(8,128)(2,1)} %param.8) | copy-start | bytes 7077892
  7.2 9.7 %copy-start.2 = (s32[2,8,2]{1,2,0:T(2,128)S(1)}, s32[2,8,2]{1,2,0:T(2,128)}, u32[]{:S(2)}) copy-start(s32[2,8,2]{1,2,0:T(2,128)} %param.10) | copy-start | bytes 388
  7.2 9.8 %copy-start.3 = (s32[2,8]{1,0:T(2,128)S(1)}, s32[2,8]{1,0:T(2,128)}, u32[]{:S(2)}) copy-start(s32[2,8]{1,0:T(2,128)} %param.11) | copy-start | bytes 196
  7.2 288.2 %all-reduce.2.cloned.1.call-start = ((), (), s32[]{:S(2)}) async-start(), calls=%async_computation | async-start | bytes 6291456 | tf_op jit(solution)/shard_map/psum | solution.py:48
  13.5 69.6 %collective-permute-start = (bf16[2,4,384,512]{3,2,1,0:T(8,128)(2,1)}, bf16[2,4,384,512]{3,2,1,0:T(8,128)(2,1)}, u32[]{:S(2)}, u32[]{:S(2)}) collective-permute-start(bf16[2,4,384,512]{3,2,1,0:T(8,128)(2,1)} %get-tuple-element.8), channel_id=1, source_target_pairs={{0,4},{4,8},{8,12},{12,16},{16,20},{20,24},{24,28},{28,0},{1,5},{5... | collective-permute-start | bytes 9437192 | tf_op jit(solution)/shard_map/ppermute | solution.py:17
  13.9 70.7 %collective-permute-start.1 = (bf16[2,4,384,512]{3,2,1,0:T(8,128)(2,1)}, bf16[2,4,384,512]{3,2,1,0:T(8,128)(2,1)}, u32[]{:S(2)}, u32[]{:S(2)}) collective-permute-start(bf16[2,4,384,512]{3,2,1,0:T(8,128)(2,1)} %get-tuple-element.9), channel_id=1, source_target_pairs={{4,0},{8,4},{12,8},{16,12},{20,16},{24,20},{28,24},{0,28},{5,1},{9... | collective-permute-start | bytes 9437192 | tf_op jit(solution)/shard_map/ppermute | solution.py:19
  130.1 177.5 %collective-permute-start.2 = (bf16[8,384,512]{1,2,0:T(8,128)(2,1)}, bf16[8,384,512]{1,2,0:T(8,128)(2,1)}, u32[]{:S(2)}, u32[]{:S(2)}) collective-permute-start(bf16[8,384,512]{1,2,0:T(8,128)(2,1)} %bitcast.25), channel_id=1, source_target_pairs={{0,1},{1,2},{2,3},{4,5},{5,6},{6,7},{8,9},{9,10},{10,11},{12,13},{... | collective-permute-start | bytes 9437192 | tf_op jit(solution)/shard_map/ppermute | solution.py:29
  307.6 2.8 copy-start.1
Sparse Core Ops, SparseCore 0:
  119.4 175.9 all-reduce.1
where the time goes:
time: 330 us; the launch traced here: 329 us
  waiting for transfers between devices  223 us (68%)
  local copies, waits for them, and re-layouts  47 us (14%)
  matrix products  20.2 us (6%)
  other arithmetic  16.4 us (5%)
  between operations  14.1 us (4%)
  starting transfers between devices  8.45 us (3%)
    psum x1, waiting for transfers between devices, shards(): lax.psum(partial_field.astype(jnp.bfloat16), 'lag').astype(jnp.float32)  156 us
    ppermute x1, waiting for transfers between devices, padded(): lax.ppermute(tail, axis, [(i, (i + 1) % count) for i in range(count)])  66 us
    unnamed x12, local copies, waits for them, and re-layouts  23.1 us
    dot_general x1, matrix products, shards(): jnp.einsum('lbsij,lbsjr->bir', lag_blocks, sources, preferred_element_typ...  12.6 us
    gather x3, local copies, waits for them, and re-layouts, pick_sources(): return window[source_index]  11.6 us
    concatenate x1, other arithmetic, padded(): jnp.concatenate([lax.ppermute(tail, axis, [(i, (i + 1) % count) for i in...  10.5 us
    dot_general x1, matrix products, shards(): jnp.einsum('bij,bjr->bir', self_inverse, residual, preferred_element_type...  7.62 us
  transfers between devices with their start and end apart: 4, of which 3 were waited for; matrix products, arithmetic and copies ran while one was open for 9% of the time, Pallas kernels for 0%

commit v1 on v0

v1 whole, which is shorter than its diff:
```python
import functools

import jax
import jax.numpy as jnp
from jax import lax
from jax.experimental import pallas as pl
from jax.experimental.pallas import tpu as pltpu
from jax.sharding import PartitionSpec as P

SLOTS = 2
EDGE = 4
COLS = 256
ROWS = 128
MESH = pl.DeviceIdType.MESH


def march(
    n_tile, n_lag,
    history, lag_blocks, self_inverse, excitation, pattern, live_counts,
    traction, shifted,
    window, land, blocks, inverse, excite, psend, inbox, resbox, tbuf,
    local_sem, halo_send, halo_recv, carry_send, carry_recv,
    in_send, in_recv, res_send, res_recv, out_sem, first_sem,
):
    lags, here, vec, width = history.shape
    tile = lax.axis_index("tile")
    lag = lax.axis_index("lag")
    half = n_lag // 2
    right, left = lax.rem(tile + 1, n_tile), lax.rem(tile + n_tile - 1, n_tile)
    left_half = lag < half
    inward = jnp.where(left_half, lag + 1, lag - 1)
    has_out = (lag > 0) & (lag < n_lag - 1)
    outward = jnp.where(has_out, jnp.where(left_half, lag - 1, lag + 1), inward)
    middle = (lag == half - 1) | (lag == half)

    def halo(k, side):
        block = here - 1 - k if side == 0 else k
        return pltpu.make_async_remote_copy(
            src_ref=history.at[:, block],
            dst_ref=land.at[k, side],
            send_sem=halo_send.at[k, side],
            recv_sem=halo_recv.at[k, side],
            device_id={"tile": right if side == 0 else left},
            device_id_type=MESH,
        )

    def carry(c):
        return pltpu.make_async_remote_copy(
            src_ref=history.at[lags - 1, c],
            dst_ref=shifted.at[0, c],
            send_sem=carry_send.at[c],
            recv_sem=carry_recv.at[c],
            device_id={"lag": lax.rem(lag + 1, n_lag)},
            device_id_type=MESH,
        )

    def to_inward(k, dst, recv):
        return pltpu.make_async_remote_copy(
            src_ref=psend.at[k],
            dst_ref=dst.at[k],
            send_sem=in_send.at[k],
            recv_sem=recv.at[k],
            device_id={"lag": inward},
            device_id_type=MESH,
        )

    def to_outward(k):
        return pltpu.make_async_remote_copy(
            src_ref=resbox.at[k],
            dst_ref=resbox.at[k],
            send_sem=res_send.at[k],
            recv_sem=res_recv.at[k],
            device_id={"lag": outward},
            device_id_type=MESH,
        )

    def target(k, side):
        return EDGE - 1 - k + side * (2 * k + 1)

    barrier = pltpu.get_barrier_semaphore()
    pl.semaphore_signal(barrier, inc=1, device_id={"tile": left}, device_id_type=MESH)
    pl.semaphore_signal(barrier, inc=1, device_id={"tile": right}, device_id_type=MESH)

    @pl.when(lag > 0)
    def _():
        pl.semaphore_signal(barrier, inc=1, device_id={"lag": lag - 1}, device_id_type=MESH)

    @pl.when(lag < n_lag - 1)
    def _():
        pl.semaphore_signal(barrier, inc=1, device_id={"lag": lag + 1}, device_id_type=MESH)

    at_end = (lag == 0) | (lag == n_lag - 1)
    pl.semaphore_wait(barrier, jnp.where(at_end, 3, 4))

    halo(0, 0).start()
    halo(0, 1).start()

    def start_carry(late):
        for c in range(here):
            early = c < 2 * (lag + 1)
            @pl.when((lag < n_lag - 1) & (~early if late else early))
            def _():
                carry(c).start()

    start_carry(False)

    loads = [
        pltpu.make_async_copy(history, window.at[:, pl.ds(EDGE, here)], local_sem.at[0]),
        pltpu.make_async_copy(lag_blocks, blocks, local_sem.at[1]),
        pltpu.make_async_copy(self_inverse, inverse, local_sem.at[2]),
        pltpu.make_async_copy(excitation, excite, local_sem.at[3]),
    ]
    for load in loads:
        load.start()
    for l in range(lags):
        @pl.loop(0, vec // ROWS)
        def _(r):
            window[l, here + 2 * EDGE, pl.ds(pl.multiple_of(r * ROWS, ROWS), ROWS)] = jnp.zeros((ROWS, width), window.dtype)
    for load in loads:
        load.wait()
    kept = pltpu.make_async_copy(
        window.at[pl.ds(0, lags - 1), pl.ds(EDGE, here)], shifted.at[pl.ds(1, lags - 1)], local_sem.at[4]
    )
    kept.start()

    def compute(k):
        halo(k, 0).wait_recv()
        halo(k, 1).wait_recv()
        if k + 1 < EDGE:
            halo(k + 1, 0).start()
            halo(k + 1, 1).start()
        for l in range(lags):
            @pl.loop(0, vec // ROWS)
            def _(r):
                rows = pl.ds(pl.multiple_of(r * ROWS, ROWS), ROWS)
                window[l, EDGE - 1 - k, rows] = land[k, 0, l, rows]
                window[l, EDGE + here + k, rows] = land[k, 1, l, rows]

        @pl.loop(0, 2 * (width // COLS))
        def _(step):
            side = step // (width // COLS)
            cols = pl.ds(pl.multiple_of(lax.rem(step, width // COLS) * COLS, COLS), COLS)
            b = target(k, side)
            lhs, rhs = [], []
            for l in range(lags):
                for s in range(SLOTS):
                    index = jnp.where(s < live_counts[l, b], b + pattern[l, b, s], here + 2 * EDGE)
                    lhs.append(blocks[l, b, s])
                    rhs.append(window[l, index, :, cols])
            term = jnp.dot(
                jnp.concatenate(lhs, axis=1), jnp.concatenate(rhs, axis=0),
                preferred_element_type=jnp.float32,
            )
            psend[k, side, :, cols] = term.astype(psend.dtype)

    def forward(k):
        @pl.when(has_out)
        def _():
            to_inward(k, inbox, in_recv).wait_recv()

            @pl.loop(0, 2 * (vec // ROWS))
            def _(step):
                side = step // (vec // ROWS)
                rows = pl.ds(pl.multiple_of(lax.rem(step, vec // ROWS) * ROWS, ROWS), ROWS)
                psend[k, side, rows] = (
                    psend[k, side, rows].astype(jnp.float32) + inbox[k, side, rows].astype(jnp.float32)
                ).astype(psend.dtype)

        @pl.when(middle)
        def _():
            to_inward(k, resbox, res_recv).start()

        @pl.when(~middle)
        def _():
            to_inward(k, inbox, in_recv).start()

    def resolve(k):
        to_outward(k).wait_recv()

        @pl.when(middle)
        def _():
            @pl.loop(0, 2 * (vec // ROWS))
            def _(step):
                side = step // (vec // ROWS)
                rows = pl.ds(pl.multiple_of(lax.rem(step, vec // ROWS) * ROWS, ROWS), ROWS)
                field = psend[k, side, rows].astype(jnp.float32) + resbox[k, side, rows].astype(jnp.float32)
                resbox[k, side, rows] = (excite[target(k, side), rows] - field).astype(resbox.dtype)

        @pl.when(has_out)
        def _():
            to_outward(k).start()

        @pl.loop(0, 2)
        def _(side):
            tbuf[k, side] = jnp.dot(
                inverse[target(k, side)], resbox[k, side], preferred_element_type=jnp.float32
            ).astype(tbuf.dtype)

        for side in range(2):
            write_out(k, side).start()

            @pl.when(lag == 0)
            def _():
                write_first(k, side).start()

    def write_out(k, side):
        return pltpu.make_async_copy(tbuf.at[k, side], traction.at[target(k, side)], out_sem.at[k, side])

    def write_first(k, side):
        return pltpu.make_async_copy(tbuf.at[k, side], shifted.at[0, target(k, side)], first_sem.at[k, side])

    order = [(compute, 0)]
    for k in range(1, EDGE):
        order += [(compute, k)]
        if k == EDGE - 1:
            order += [(resolve, 0)]
        order += [(forward, k - 1)]
    order += [(resolve, 1), (forward, EDGE - 1)]
    for step, k in order:
        step(k)

    @pl.when(left_half)
    def _():
        start_carry(True)

    for k in range(2, EDGE):
        resolve(k)

    @pl.when(~left_half)
    def _():
        start_carry(True)

    kept.wait()
    for k in range(EDGE):
        for side in range(2):
            halo(k, side).wait_send()
            write_out(k, side).wait()

            @pl.when(lag == 0)
            def _():
                write_first(k, side).wait()

        to_inward(k, inbox, in_recv).wait_send()

        @pl.when(has_out)
        def _():
            to_outward(k).wait_send()

    for c in range(here):
        @pl.when(lag < n_lag - 1)
        def _():
            carry(c).wait_send()

        @pl.when(lag > 0)
        def _():
            carry(c).wait_recv()


def shards(n_tile, n_lag, history, lag_blocks, self_inverse, excitation, pattern, live_counts):
    lags, here, vec, width = history.shape
    kind = history.dtype
    anywhere = pl.BlockSpec(memory_space=pl.ANY)
    scalars = pl.BlockSpec(memory_space=pltpu.SMEM)
    dma = pltpu.SemaphoreType.DMA
    pair = (EDGE, 2, vec, width)
    flops = 2 * here * vec * vec * width * (lags * SLOTS + 1)
    return pl.pallas_call(
        functools.partial(march, n_tile, n_lag),
        out_shape=(
            jax.ShapeDtypeStruct((here, vec, width), kind),
            jax.ShapeDtypeStruct((lags, here, vec, width), kind),
        ),
        in_specs=[anywhere] * 4 + [scalars] * 2,
        out_specs=(anywhere, anywhere),
        scratch_shapes=[
            pltpu.VMEM((lags, here + 2 * EDGE + 1, vec, width), kind),
            pltpu.VMEM((EDGE, 2, lags, vec, width), kind),
            pltpu.VMEM(lag_blocks.shape, kind),
            pltpu.VMEM(self_inverse.shape, kind),
            pltpu.VMEM(excitation.shape, excitation.dtype),
            pltpu.VMEM(pair, kind),
            pltpu.VMEM(pair, kind),
            pltpu.VMEM(pair, kind),
            pltpu.VMEM(pair, kind),
            dma((5,)),
            dma((EDGE, 2)), dma((EDGE, 2)),
            dma((here,)), dma((here,)),
            dma((EDGE,)), dma((EDGE,)),
            dma((EDGE,)), dma((EDGE,)),
            dma((EDGE, 2)), dma((EDGE, 2)),
        ],
        compiler_params=pltpu.CompilerParams(
            collective_id=0, has_side_effects=True, vmem_limit_bytes=60 * 2**20
        ),
        cost_estimate=pl.CostEstimate(flops=flops, bytes_accessed=40 * 2**20, transcendentals=0),
    )(history, lag_blocks, self_inverse, excitation, pattern, live_counts)


def solution(mesh):
    in_specs = (
        P("lag", "tile", None, None),
        P("lag", "tile", None, None, None),
        P("tile", None, None),
        P("tile", None, None),
        P("lag", "tile", None),
        P("lag", "tile"),
    )
    out_specs = (P("tile", None, None), P("lag", "tile", None, None))
    body = functools.partial(shards, mesh.shape["tile"], mesh.shape["lag"])
    return jax.shard_map(body, mesh=mesh, in_specs=in_specs, out_specs=out_specs, check_vma=False)
```

time: 330 us -> 218 us (0.66)
  waiting for transfers between devices: 223 us -> 0 us
  Pallas kernels: 0 us -> 208 us
  local copies, waits for them, and re-layouts: 47 us -> 8.92 us
  matrix products: 20.2 us -> 0 us
  other arithmetic: 16.4 us -> 0 us
  between operations: 14.1 us -> 0.65 us
  starting transfers between devices: 8.45 us -> 0 us
    pallas_call x0 -> x1, Pallas kernels: none -> 208 us  [shards(): pl.pallas_call(functools.partial(march, n_tile, n_lag), out_shape=(jax.Sh...]
    psum x1 -> x0, waiting for transfers between devices: 156 us -> none  [shards(): lax.psum(partial_field.astype(jnp.bfloat16), 'lag').astype(jnp.float32)]
    ppermute x3 -> x0, waiting for transfers between devices: 67.6 us -> none  [the longest x1 66 us: padded(): lax.ppermute(tail, axis, [(i, (i + 1) % count) for i in range(count)])]
    dot_general x2 -> x0, matrix products: 20.2 us -> none  [the longest x1 12.6 us: shards(): jnp.einsum('lbsij,lbsjr->bir', lag_blocks, sources, preferred_element_typ...]
    unnamed x12 -> x5, local copies, waits for them, and re-layouts: 23.1 us -> 8.92 us
    concatenate x2 -> x0, other arithmetic: 13.9 us -> none  [the longest x1 10.5 us: padded(): jnp.concatenate([lax.ppermute(tail, axis, [(i, (i + 1) % count) for i in...]
    slice x2 -> x0, local copies, waits for them, and re-layouts: 12.3 us -> none  [the longest x1 6.25 us: padded(): lax.slice_in_dim(cells, cells.shape[dim] - width, cells.shape[dim], axis=...]
    gather x3 -> x0, local copies, waits for them, and re-layouts: 11.6 us -> none  [pick_sources(): return window[source_index]]
  transfers between devices with their start and end apart: 4 -> 0, of which waited for: 3 -> 0; matrix products, arithmetic and copies ran while one was open for 9% -> 0% of each run, Pallas kernels for 0% -> 0%
where the time goes in v1:
time: 218 us; the launch traced here: 217 us
  Pallas kernels  208 us (95%)
  local copies, waits for them, and re-layouts  8.92 us (4%)
    pallas_call x1, Pallas kernels, shards(): pl.pallas_call(functools.partial(march, n_tile, n_lag), out_shape=(jax.Sh...  208 us
    unnamed x5, local copies, waits for them, and re-layouts  8.92 us

profile of v1, /device:TPU:0, one launch (start us, length us, event | category | flops | bytes accessed | tf_op | source)
XLA Modules:
  0.0 217.3 jit_solution(6227150285880429102)
XLA Ops:
  0.6 1.4 copy.8.pattern
  2.0 207.7 %shard_map.77 = (bf16[8,384,512]{2,1,0:T(8,128)(2,1)}, bf16[2,8,384,512]{3,2,1,0:T(8,128)(2,1)}) custom-call(bf16[2,8,384,512]{3,2,1,0:T(8,128)(2,1)} %history.1, bf16[2,8,2,384,384]{4,3,2,1,0:T(8,128)(2,1)} %lag_blocks.1, bf16[8,384,384]{2,1,0:T(8,128)(2,1)} %self_inverse.1, f32[8,384,512]{2,1,0:T(8,128)} %excitation.1, s32[2,8,2]{2,1,0:T(8,128)} %copy.8.pattern, ...), custom_call_target="tpu_custom_call" | custom-call | flops 6039797760 | bytes 41943040 | tf_op jit(solution)/shard_map/pallas_call | solution.py:267
  209.7 0.0 copy-start
  209.7 3.9 %copy.11 = bf16[8,384,512]{2,1,0:T(8,128)(2,1)} copy(bf16[8,384,512]{2,1,0:T(8,128)(2,1)} %get-tuple-element.4) | data formatting | bytes 6291456
  213.7 0.9 copy-done
  214.6 2.7 %copy.12 = bf16[2,8,384,512]{3,2,1,0:T(8,128)(2,1)} copy(bf16[2,8,384,512]{3,2,1,0:T(8,128)(2,1)S(1)} %copy-done) | data formatting | bytes 12582912
Async XLA Ops:
  209.7 4.9 %copy-start = (bf16[2,8,384,512]{3,2,1,0:T(8,128)(2,1)S(1)}, bf16[2,8,384,512]{3,2,1,0:T(8,128)(2,1)}, u32[]{:S(2)}) copy-start(bf16[2,8,384,512]{3,2,1,0:T(8,128)(2,1)} %get-tuple-element.5) | copy-start | bytes 18874372

commit v2 on v1

v2 whole, which is shorter than its diff:
```python
import functools

import jax
import jax.numpy as jnp
from jax import lax
from jax.experimental import pallas as pl
from jax.experimental.pallas import tpu as pltpu
from jax.sharding import PartitionSpec as P

SLOTS = 2
EDGE = 4
COLS = 256
ROWS = 128
MESH = pl.DeviceIdType.MESH


def march(
    n_tile, n_lag,
    history, lag_blocks, self_inverse, excitation, pattern, live_counts,
    traction, shifted,
    window, land, blocks, inverse, excite, psend, inbox, resbox, tbuf,
    local_sem, halo_send, halo_recv, carry_send, carry_recv,
    in_send, in_recv, res_send, res_recv, out_sem, first_sem,
):
    lags, here, vec, width = history.shape
    tile = lax.axis_index("tile")
    lag = lax.axis_index("lag")
    half = n_lag // 2
    right, left = lax.rem(tile + 1, n_tile), lax.rem(tile + n_tile - 1, n_tile)
    left_half = lag < half
    inward = jnp.where(left_half, lag + 1, lag - 1)
    has_out = (lag > 0) & (lag < n_lag - 1)
    outward = jnp.where(has_out, jnp.where(left_half, lag - 1, lag + 1), inward)
    middle = (lag == half - 1) | (lag == half)

    def halo(k, side, l):
        block = here - 1 - k if side == 0 else k
        return pltpu.make_async_remote_copy(
            src_ref=history.at[l, block],
            dst_ref=land.at[k, side, l],
            send_sem=halo_send.at[k, side, l],
            recv_sem=halo_recv.at[k, side, l],
            device_id={"tile": right if side == 0 else left},
            device_id_type=MESH,
        )

    def carry(c):
        return pltpu.make_async_remote_copy(
            src_ref=history.at[lags - 1, c],
            dst_ref=shifted.at[0, c],
            send_sem=carry_send.at[c],
            recv_sem=carry_recv.at[c],
            device_id={"lag": lax.rem(lag + 1, n_lag)},
            device_id_type=MESH,
        )

    def to_inward(k, side, dst, recv):
        return pltpu.make_async_remote_copy(
            src_ref=psend.at[k, side],
            dst_ref=dst.at[k, side],
            send_sem=in_send.at[k, side],
            recv_sem=recv.at[k, side],
            device_id={"lag": inward},
            device_id_type=MESH,
        )

    def to_outward(k, side):
        return pltpu.make_async_remote_copy(
            src_ref=resbox.at[k, side],
            dst_ref=resbox.at[k, side],
            send_sem=res_send.at[k, side],
            recv_sem=res_recv.at[k, side],
            device_id={"lag": outward},
            device_id_type=MESH,
        )

    def target(k, side):
        return EDGE - 1 - k + side * (2 * k + 1)

    barrier = pltpu.get_barrier_semaphore()
    pl.semaphore_signal(barrier, inc=1, device_id={"tile": left}, device_id_type=MESH)
    pl.semaphore_signal(barrier, inc=1, device_id={"tile": right}, device_id_type=MESH)

    @pl.when(lag > 0)
    def _():
        pl.semaphore_signal(barrier, inc=1, device_id={"lag": lag - 1}, device_id_type=MESH)

    @pl.when(lag < n_lag - 1)
    def _():
        pl.semaphore_signal(barrier, inc=1, device_id={"lag": lag + 1}, device_id_type=MESH)

    at_end = (lag == 0) | (lag == n_lag - 1)
    pl.semaphore_wait(barrier, jnp.where(at_end, 3, 4))

    for l in range(lags):
        for side in range(2):
            halo(0, side, l).start()

    def is_early(c):
        return (c < 2 * (lag + 2)) | ~left_half

    for c in range(here):
        @pl.when((lag < n_lag - 1) & is_early(c))
        def _():
            carry(c).start()

    def start_late(part):
        for c in range(part, here, 2):
            @pl.when((lag < n_lag - 1) & ~is_early(c))
            def _():
                carry(c).start()

    loads = [
        pltpu.make_async_copy(history, window.at[:, pl.ds(EDGE, here)], local_sem.at[0]),
        pltpu.make_async_copy(lag_blocks, blocks, local_sem.at[1]),
        pltpu.make_async_copy(self_inverse, inverse, local_sem.at[2]),
        pltpu.make_async_copy(excitation, excite, local_sem.at[3]),
    ]
    for load in loads:
        load.start()
    for l in range(lags):
        @pl.loop(0, vec // ROWS)
        def _(r):
            window[l, here + 2 * EDGE, pl.ds(pl.multiple_of(r * ROWS, ROWS), ROWS)] = jnp.zeros((ROWS, width), window.dtype)
    for load in loads:
        load.wait()
    kept = pltpu.make_async_copy(
        window.at[pl.ds(0, lags - 1), pl.ds(EDGE, here)], shifted.at[pl.ds(1, lags - 1)], local_sem.at[4]
    )
    kept.start()

    def compute(k):
        for l in range(lags):
            for side in range(2):
                halo(k, side, l).wait_recv()
                if k + 1 < EDGE:
                    halo(k + 1, side, l).start()
        for l in range(lags):
            @pl.loop(0, vec // ROWS)
            def _(r):
                rows = pl.ds(pl.multiple_of(r * ROWS, ROWS), ROWS)
                window[l, EDGE - 1 - k, rows] = land[k, 0, l, rows]
                window[l, EDGE + here + k, rows] = land[k, 1, l, rows]

        for side in range(2):
            b = target(k, side)

            @pl.loop(0, width // COLS)
            def _(c):
                cols = pl.ds(pl.multiple_of(c * COLS, COLS), COLS)
                lhs, rhs = [], []
                for l in range(lags):
                    for s in range(SLOTS):
                        index = jnp.where(s < live_counts[l, b], b + pattern[l, s, b], here + 2 * EDGE)
                        lhs.append(blocks[l, b, s])
                        rhs.append(window[l, index, :, cols])
                term = jnp.dot(
                    jnp.concatenate(lhs, axis=1), jnp.concatenate(rhs, axis=0),
                    preferred_element_type=jnp.float32,
                )
                psend[k, side, :, cols] = term.astype(psend.dtype)

            @pl.when(~has_out)
            def _():
                send_inward(k, side)

    def send_inward(k, side):
        @pl.when(middle)
        def _():
            to_inward(k, side, resbox, res_recv).start()

        @pl.when(~middle)
        def _():
            to_inward(k, side, inbox, in_recv).start()

    def forward(k):
        @pl.when(has_out)
        def _():
            for side in range(2):
                to_inward(k, side, inbox, in_recv).wait_recv()

                @pl.loop(0, vec // ROWS)
                def _(r):
                    rows = pl.ds(pl.multiple_of(r * ROWS, ROWS), ROWS)
                    psend[k, side, rows] = (
                        psend[k, side, rows].astype(jnp.float32) + inbox[k, side, rows].astype(jnp.float32)
                    ).astype(psend.dtype)

                send_inward(k, side)

    def resolve(k, side):
        to_outward(k, side).wait_recv()

        @pl.when(middle)
        def _():
            @pl.loop(0, vec // ROWS)
            def _(r):
                rows = pl.ds(pl.multiple_of(r * ROWS, ROWS), ROWS)
                field = psend[k, side, rows].astype(jnp.float32) + resbox[k, side, rows].astype(jnp.float32)
                resbox[k, side, rows] = (excite[target(k, side), rows] - field).astype(resbox.dtype)

        @pl.when(has_out)
        def _():
            to_outward(k, side).start()

        tbuf[k, side] = jnp.dot(
            inverse[target(k, side)], resbox[k, side], preferred_element_type=jnp.float32
        ).astype(tbuf.dtype)
        write_out(k, side).start()

        @pl.when(lag == 0)
        def _():
            write_first(k, side).start()

    def write_out(k, side):
        return pltpu.make_async_copy(tbuf.at[k, side], traction.at[target(k, side)], out_sem.at[k, side])

    def write_first(k, side):
        return pltpu.make_async_copy(tbuf.at[k, side], shifted.at[0, target(k, side)], first_sem.at[k, side])

    def resolve_middle(k):
        @pl.when(middle)
        def _():
            for side in range(2):
                resolve(k, side)
                if k == EDGE - 1:
                    start_late(side)

    for k in range(EDGE):
        if k == EDGE - 1:
            resolve_middle(0)
        compute(k)
        if k > 0:
            forward(k - 1)
    resolve_middle(1)
    forward(EDGE - 1)
    for k in range(2, EDGE):
        resolve_middle(k)

    @pl.when(~middle)
    def _():
        for side in range(2):
            to_inward(EDGE - 1, side, inbox, in_recv).wait_send()
            start_late(side)
        for k in range(EDGE):
            for side in range(2):
                resolve(k, side)

    kept.wait()
    for k in range(EDGE):
        for side in range(2):
            for l in range(lags):
                halo(k, side, l).wait_send()
            write_out(k, side).wait()

            @pl.when(lag == 0)
            def _():
                write_first(k, side).wait()

            if k < EDGE - 1:
                to_inward(k, side, inbox, in_recv).wait_send()
            else:
                @pl.when(middle)
                def _():
                    to_inward(k, side, inbox, in_recv).wait_send()

            @pl.when(has_out)
            def _():
                to_outward(k, side).wait_send()

    for c in range(here):
        @pl.when(lag < n_lag - 1)
        def _():
            carry(c).wait_send()

        @pl.when(lag > 0)
        def _():
            carry(c).wait_recv()


def shards(n_tile, n_lag, history, lag_blocks, self_inverse, excitation, pattern, live_counts):
    lags, here, vec, width = history.shape
    kind = history.dtype
    anywhere = pl.BlockSpec(memory_space=pl.ANY)
    scalars = pl.BlockSpec(memory_space=pltpu.SMEM)
    dma = pltpu.SemaphoreType.DMA
    pair = (EDGE, 2, vec, width)
    flops = 2 * here * vec * vec * width * (lags * SLOTS + 1)
    return pl.pallas_call(
        functools.partial(march, n_tile, n_lag),
        out_shape=(
            jax.ShapeDtypeStruct((here, vec, width), kind),
            jax.ShapeDtypeStruct((lags, here, vec, width), kind),
        ),
        in_specs=[anywhere] * 4 + [scalars] * 2,
        out_specs=(anywhere, anywhere),
        scratch_shapes=[
            pltpu.VMEM((lags, here + 2 * EDGE + 1, vec, width), kind),
            pltpu.VMEM((EDGE, 2, lags, vec, width), kind),
            pltpu.VMEM(lag_blocks.shape, kind),
            pltpu.VMEM(self_inverse.shape, kind),
            pltpu.VMEM(excitation.shape, excitation.dtype),
            pltpu.VMEM(pair, kind),
            pltpu.VMEM(pair, kind),
            pltpu.VMEM(pair, kind),
            pltpu.VMEM(pair, kind),
            dma((5,)),
            dma((EDGE, 2, lags)), dma((EDGE, 2, lags)),
            dma((here,)), dma((here,)),
            dma((EDGE, 2)), dma((EDGE, 2)),
            dma((EDGE, 2)), dma((EDGE, 2)),
            dma((EDGE, 2)), dma((EDGE, 2)),
        ],
        compiler_params=pltpu.CompilerParams(
            collective_id=0, has_side_effects=True, vmem_limit_bytes=60 * 2**20
        ),
        cost_estimate=pl.CostEstimate(flops=flops, bytes_accessed=40 * 2**20, transcendentals=0),
    )(history, lag_blocks, self_inverse, excitation, jnp.swapaxes(pattern, 1, 2), live_counts)


def solution(mesh):
    in_specs = (
        P("lag", "tile", None, None),
        P("lag", "tile", None, None, None),
        P("tile", None, None),
        P("tile", None, None),
        P("lag", "tile", None),
        P("lag", "tile"),
    )
    out_specs = (P("tile", None, None), P("lag", "tile", None, None))
    body = functools.partial(shards, mesh.shape["tile"], mesh.shape["lag"])
    return jax.shard_map(body, mesh=mesh, in_specs=in_specs, out_specs=out_specs, check_vma=False)
```

time: 218 us -> 153 us (0.70)
  Pallas kernels: 208 us -> 144 us
    pallas_call x1, Pallas kernels: 208 us -> 144 us  [shards(): pl.pallas_call(functools.partial(march, n_tile, n_lag), out_shape=(jax.Sh...]
    unnamed x5 -> x4, local copies, waits for them, and re-layouts: 8.92 us -> 7.56 us
where the time goes in v2:
time: 153 us; the launch traced here: 152 us
  Pallas kernels  144 us (94%)
  local copies, waits for them, and re-layouts  7.56 us (5%)
    pallas_call x1, Pallas kernels, shards(): pl.pallas_call(functools.partial(march, n_tile, n_lag), out_shape=(jax.Sh...  144 us
    unnamed x4, local copies, waits for them, and re-layouts  7.56 us

profile of v2, /device:TPU:0, one launch (start us, length us, event | category | flops | bytes accessed | tf_op | source)
XLA Modules:
  0.0 152.3 jit_solution(15625400834368347647)
XLA Ops:
  0.6 144.1 %shard_map.77 = (bf16[8,384,512]{2,1,0:T(8,128)(2,1)}, bf16[2,8,384,512]{3,2,1,0:T(8,128)(2,1)}) custom-call(bf16[2,8,384,512]{3,2,1,0:T(8,128)(2,1)} %history.1, bf16[2,8,2,384,384]{4,3,2,1,0:T(8,128)(2,1)} %lag_blocks.1, bf16[8,384,384]{2,1,0:T(8,128)(2,1)} %self_inverse.1, f32[8,384,512]{2,1,0:T(8,128)} %excitation.1, s32[2,2,8]{2,1,0:T(2,128)} %bitcast.1, ...), custom_call_target="tpu_custom_call" | custom-call | flops 6039797760 | bytes 41943040 | tf_op jit(solution)/shard_map/pallas_call | solution.py:289
  144.8 0.0 copy-start
  144.8 3.9 %copy.10 = bf16[8,384,512]{2,1,0:T(8,128)(2,1)} copy(bf16[8,384,512]{2,1,0:T(8,128)(2,1)} %get-tuple-element.4) | data formatting | bytes 6291456
  148.7 0.9 copy-done
  149.6 2.7 %copy.11 = bf16[2,8,384,512]{3,2,1,0:T(8,128)(2,1)} copy(bf16[2,8,384,512]{3,2,1,0:T(8,128)(2,1)S(1)} %copy-done) | data formatting | bytes 12582912
Async XLA Ops:
  144.8 4.9 %copy-start = (bf16[2,8,384,512]{3,2,1,0:T(8,128)(2,1)S(1)}, bf16[2,8,384,512]{3,2,1,0:T(8,128)(2,1)}, u32[]{:S(2)}) copy-start(bf16[2,8,384,512]{3,2,1,0:T(8,128)(2,1)} %get-tuple-element.5) | copy-start | bytes 18874372

commit v3 on v2

--- a/solution.py
+++ b/solution.py
@@ -17,10 +17,10 @@
 def march(
     n_tile, n_lag,
     history, lag_blocks, self_inverse, excitation, pattern, live_counts,
-    traction, shifted,
-    window, land, blocks, inverse, excite, psend, inbox, resbox, tbuf,
+    traction, newest, older,
+    window, land, blocks, inverse, excite, psend, inbox, resbox,
     local_sem, halo_send, halo_recv, carry_send, carry_recv,
-    in_send, in_recv, res_send, res_recv, out_sem, first_sem,
+    in_send, in_recv, res_send, res_recv,
 ):
     lags, here, vec, width = history.shape
     tile = lax.axis_index("tile")
@@ -47,7 +47,7 @@
     def carry(c):
         return pltpu.make_async_remote_copy(
             src_ref=history.at[lags - 1, c],
-            dst_ref=shifted.at[0, c],
+            dst_ref=newest.at[c],
             send_sem=carry_send.at[c],
             recv_sem=carry_recv.at[c],
             device_id={"lag": lax.rem(lag + 1, n_lag)},
@@ -92,10 +92,6 @@
     at_end = (lag == 0) | (lag == n_lag - 1)
     pl.semaphore_wait(barrier, jnp.where(at_end, 3, 4))
 
-    for l in range(lags):
-        for side in range(2):
-            halo(0, side, l).start()
-
     def is_early(c):
         return (c < 2 * (lag + 2)) | ~left_half
 
@@ -103,6 +99,10 @@
         @pl.when((lag < n_lag - 1) & is_early(c))
         def _():
             carry(c).start()
+
+    for l in range(lags):
+        for side in range(2):
+            halo(0, side, l).start()
 
     def start_late(part):
         for c in range(part, here, 2):
@@ -125,7 +125,7 @@
     for load in loads:
         load.wait()
     kept = pltpu.make_async_copy(
-        window.at[pl.ds(0, lags - 1), pl.ds(EDGE, here)], shifted.at[pl.ds(1, lags - 1)], local_sem.at[4]
+        window.at[pl.ds(0, lags - 1), pl.ds(EDGE, here)], older, local_sem.at[4]
     )
     kept.start()
 
@@ -173,20 +173,19 @@
         def _():
             to_inward(k, side, inbox, in_recv).start()
 
-    def forward(k):
+    def forward(k, side):
         @pl.when(has_out)
         def _():
-            for side in range(2):
-                to_inward(k, side, inbox, in_recv).wait_recv()
-
-                @pl.loop(0, vec // ROWS)
-                def _(r):
-                    rows = pl.ds(pl.multiple_of(r * ROWS, ROWS), ROWS)
-                    psend[k, side, rows] = (
-                        psend[k, side, rows].astype(jnp.float32) + inbox[k, side, rows].astype(jnp.float32)
-                    ).astype(psend.dtype)
-
-                send_inward(k, side)
+            to_inward(k, side, inbox, in_recv).wait_recv()
+
+            @pl.loop(0, vec // ROWS)
+            def _(r):
+                rows = pl.ds(pl.multiple_of(r * ROWS, ROWS), ROWS)
+                psend[k, side, rows] = (
+                    psend[k, side, rows].astype(jnp.float32) + inbox[k, side, rows].astype(jnp.float32)
+                ).astype(psend.dtype)
+
+            send_inward(k, side)
 
     def resolve(k, side):
         to_outward(k, side).wait_recv()
@@ -203,39 +202,32 @@
         def _():
             to_outward(k, side).start()
 
-        tbuf[k, side] = jnp.dot(
+        traction[target(k, side)] = jnp.dot(
             inverse[target(k, side)], resbox[k, side], preferred_element_type=jnp.float32
-        ).astype(tbuf.dtype)
-        write_out(k, side).start()
-
-        @pl.when(lag == 0)
-        def _():
-            write_first(k, side).start()
-
-    def write_out(k, side):
-        return pltpu.make_async_copy(tbuf.at[k, side], traction.at[target(k, side)], out_sem.at[k, side])
-
-    def write_first(k, side):
-        return pltpu.make_async_copy(tbuf.at[k, side], shifted.at[0, target(k, side)], first_sem.at[k, side])
-
-    def resolve_middle(k):
+        ).astype(traction.dtype)
+
+    def resolve_middle(k, side):
         @pl.when(middle)
         def _():
-            for side in range(2):
-                resolve(k, side)
-                if k == EDGE - 1:
-                    start_late(side)
+            resolve(k, side)
+            if k == EDGE - 1:
+                start_late(side)
 
     for k in range(EDGE):
         if k == EDGE - 1:
-            resolve_middle(0)
+            for side in range(2):
+                resolve_middle(0, side)
         compute(k)
-        if k > 0:
-            forward(k - 1)
-    resolve_middle(1)
-    forward(EDGE - 1)
-    for k in range(2, EDGE):
-        resolve_middle(k)
+        for side in range(2):
+            if k == EDGE - 1:
+                resolve_middle(1, side)
+            if k > 0:
+                forward(k - 1, side)
+    for side in range(2):
+        resolve_middle(2, side)
+        forward(EDGE - 1, side)
+    for side in range(2):
+        resolve_middle(EDGE - 1, side)
 
     @pl.when(~middle)
     def _():
@@ -251,12 +243,6 @@
         for side in range(2):
             for l in range(lags):
                 halo(k, side, l).wait_send()
-            write_out(k, side).wait()
-
-            @pl.when(lag == 0)
-            def _():
-                write_first(k, side).wait()
-
             if k < EDGE - 1:
                 to_inward(k, side, inbox, in_recv).wait_send()
             else:
@@ -276,6 +262,28 @@
         @pl.when(lag > 0)
         def _():
             carry(c).wait_recv()
+
+
+def place(traction, newest, older, traction_out, shifted_out, sem):
+    lags, here = shifted_out.shape[:2]
+    first = lax.axis_index("lag") == 0
+    for c in range(here):
+        pltpu.make_async_copy(traction.at[c], traction_out.at[c], sem.at[0, c]).start()
+        for l in range(1, lags):
+            pltpu.make_async_copy(older.at[l - 1, c], shifted_out.at[l, c], sem.at[l + 1, c]).start()
+
+        @pl.when(first)
+        def _():
+            pltpu.make_async_copy(traction.at[c], shifted_out.at[0, c], sem.at[1, c]).start()
+
+        @pl.when(~first)
+        def _():
+            pltpu.make_async_copy(newest.at[c], shifted_out.at[0, c], sem.at[1, c]).start()
+
+    for c in range(here):
+        pltpu.make_async_copy(traction.at[c], traction_out.at[c], sem.at[0, c]).wait()
+        for l in range(lags):
+            pltpu.make_async_copy(traction.at[c], shifted_out.at[l, c], sem.at[l + 1, c]).wait()
 
 
 def shards(n_tile, n_lag, history, lag_blocks, self_inverse, excitation, pattern, live_counts):
@@ -286,14 +294,15 @@
     dma = pltpu.SemaphoreType.DMA
     pair = (EDGE, 2, vec, width)
     flops = 2 * here * vec * vec * width * (lags * SLOTS + 1)
-    return pl.pallas_call(
+    traction, newest, older = pl.pallas_call(
         functools.partial(march, n_tile, n_lag),
         out_shape=(
-            jax.ShapeDtypeStruct((here, vec, width), kind),
-            jax.ShapeDtypeStruct((lags, here, vec, width), kind),
+            pltpu.VMEM((here, vec, width), kind),
+            pltpu.VMEM((here, vec, width), kind),
+            pltpu.VMEM((lags - 1, here, vec, width), kind),
         ),
         in_specs=[anywhere] * 4 + [scalars] * 2,
-        out_specs=(anywhere, anywhere),
+        out_specs=(pl.BlockSpec(memory_space=pltpu.VMEM), anywhere, anywhere),
         scratch_shapes=[
             pltpu.VMEM((lags, here + 2 * EDGE + 1, vec, width), kind),
             pltpu.VMEM((EDGE, 2, lags, vec, width), kind),
@@ -303,19 +312,28 @@
             pltpu.VMEM(pair, kind),
             pltpu.VMEM(pair, kind),
             pltpu.VMEM(pair, kind),
-            pltpu.VMEM(pair, kind),
             dma((5,)),
             dma((EDGE, 2, lags)), dma((EDGE, 2, lags)),
             dma((here,)), dma((here,)),
             dma((EDGE, 2)), dma((EDGE, 2)),
             dma((EDGE, 2)), dma((EDGE, 2)),
-            dma((EDGE, 2)), dma((EDGE, 2)),
         ],
         compiler_params=pltpu.CompilerParams(
-            collective_id=0, has_side_effects=True, vmem_limit_bytes=60 * 2**20
+            collective_id=0, has_side_effects=True, vmem_limit_bytes=54 * 2**20
         ),
         cost_estimate=pl.CostEstimate(flops=flops, bytes_accessed=40 * 2**20, transcendentals=0),
     )(history, lag_blocks, self_inverse, excitation, jnp.swapaxes(pattern, 1, 2), live_counts)
+    return pl.pallas_call(
+        place,
+        out_shape=(
+            jax.ShapeDtypeStruct((here, vec, width), kind),
+            jax.ShapeDtypeStruct((lags, here, vec, width), kind),
+        ),
+        in_specs=[anywhere] * 3,
+        out_specs=(anywhere, anywhere),
+        scratch_shapes=[dma((lags + 1, here))],
+        cost_estimate=pl.CostEstimate(flops=0, bytes_accessed=16 * 2**20, transcendentals=0),
+    )(traction, newest, older)
 
 
 def solution(mesh):

time: 153 us -> 436 us (2.85)
  Pallas kernels: 144 us -> 430 us
    pallas_call x1 -> x2, Pallas kernels: 144 us -> 430 us  [the longest x1 287 us: shards(): pl.pallas_call(place, out_shape=(jax.ShapeDtypeStruct((here, vec, width),...]
where the time goes in v3:
time: 436 us
  Pallas kernels  430 us (99%)
  local copies, waits for them, and re-layouts  5 us (1%)
    pallas_call x1, Pallas kernels, shards(): pl.pallas_call(place, out_shape=(jax.ShapeDtypeStruct((here, vec, width),...  287 us
    pallas_call x1, Pallas kernels, shards(): pl.pallas_call(functools.partial(march, n_tile, n_lag), out_shape=(pltpu....  143 us

profile of v3, /device:TPU:0, one launch (start us, length us, event | category | flops | bytes accessed | tf_op | source)
XLA Modules:
  0.0 436.0 jit_solution(11931242069910478798)
XLA Ops:
  0.6 143.2 %shard_map.77 = (bf16[8,384,512]{2,1,0:T(8,128)(2,1)S(1)}, bf16[8,384,512]{2,1,0:T(8,128)(2,1)S(1)}, bf16[1,8,384,512]{3,2,1,0:T(8,128)(2,1)S(1)}) custom-call(bf16[2,8,384,512]{3,2,1,0:T(8,128)(2,1)} %history.1, bf16[2,8,2,384,384]{4,3,2,1,0:T(8,128)(2,1)} %lag_blocks.1, bf16[8,384,384]{2,1,0:T(8,128)(2,1)} %self_inverse.1, f32[8,384,512]{2,1,0:T(8,128)} %excitation.1, ...), custom_call_target="tpu_custom_call" | custom-call | flops 6039797760 | bytes 41943040 | tf_op jit(solution)/shard_map/pallas_call | solution.py:297
  143.8 0.0 copy-start
  143.8 1.6 copy-done
  145.5 0.0 copy-start.1
  145.5 1.7 copy-done.1
  147.1 0.0 copy-start.2
  147.1 1.7 copy-done.2
  148.8 287.2 %shard_map.78 = (bf16[8,384,512]{2,1,0:T(8,128)(2,1)}, bf16[2,8,384,512]{3,2,1,0:T(8,128)(2,1)}) custom-call(bf16[8,384,512]{2,1,0:T(8,128)(2,1)} %copy-done, bf16[8,384,512]{2,1,0:T(8,128)(2,1)} %copy-done.1, bf16[1,8,384,512]{3,2,1,0:T(8,128)(2,1)} %copy-done.2), custom_call_target="tpu_custom_call" | custom-call | bytes 16777216 | tf_op jit(solution)/shard_map/pallas_call | solution.py:326
Async XLA Ops:
  143.8 1.6 copy-start
  145.5 1.7 copy-start.1
  147.1 1.7 copy-start.2

commit v4 on v3

--- a/solution.py
+++ b/solution.py
@@ -210,8 +210,9 @@
         @pl.when(middle)
         def _():
             resolve(k, side)
-            if k == EDGE - 1:
-                start_late(side)
+            if k == EDGE - 1 and side == 1:
+                start_late(0)
+                start_late(1)
 
     for k in range(EDGE):
         if k == EDGE - 1:
@@ -329,9 +330,10 @@
             jax.ShapeDtypeStruct((here, vec, width), kind),
             jax.ShapeDtypeStruct((lags, here, vec, width), kind),
         ),
-        in_specs=[anywhere] * 3,
+        in_specs=[pl.BlockSpec(memory_space=pltpu.VMEM)] * 3,
         out_specs=(anywhere, anywhere),
         scratch_shapes=[dma((lags + 1, here))],
+        compiler_params=pltpu.CompilerParams(vmem_limit_bytes=32 * 2**20),
         cost_estimate=pl.CostEstimate(flops=0, bytes_accessed=16 * 2**20, transcendentals=0),
     )(traction, newest, older)
 

time: 436 us -> 148 us (0.34)
  Pallas kernels: 430 us -> 147 us
  local copies, waits for them, and re-layouts: 5 us -> 0 us
    pallas_call x1, Pallas kernels: 287 us -> 3.8 us  [shards(): pl.pallas_call(place, out_shape=(jax.ShapeDtypeStruct((here, vec, width),...]
    unnamed x6 -> x0, local copies, waits for them, and re-layouts: 5 us -> none
where the time goes in v4:
time: 148 us
  Pallas kernels  147 us (99%)
    pallas_call x1, Pallas kernels, shards(): pl.pallas_call(functools.partial(march, n_tile, n_lag), out_shape=(pltpu....  143 us
    pallas_call x1, Pallas kernels, shards(): pl.pallas_call(place, out_shape=(jax.ShapeDtypeStruct((here, vec, width),...  3.8 us

profile of v4, /device:TPU:0, one launch (start us, length us, event | category | flops | bytes accessed | tf_op | source)
XLA Modules:
  0.0 147.6 jit_solution(7606791962615279119)
XLA Ops:
  0.6 143.2 %shard_map.77 = (bf16[8,384,512]{2,1,0:T(8,128)(2,1)S(1)}, bf16[8,384,512]{2,1,0:T(8,128)(2,1)S(1)}, bf16[1,8,384,512]{3,2,1,0:T(8,128)(2,1)S(1)}) custom-call(bf16[2,8,384,512]{3,2,1,0:T(8,128)(2,1)} %history.1, bf16[2,8,2,384,384]{4,3,2,1,0:T(8,128)(2,1)} %lag_blocks.1, bf16[8,384,384]{2,1,0:T(8,128)(2,1)} %self_inverse.1, f32[8,384,512]{2,1,0:T(8,128)} %excitation.1, ...), custom_call_target="tpu_custom_call" | custom-call | flops 6039797760 | bytes 41943040 | tf_op jit(solution)/shard_map/pallas_call | solution.py:298
  143.8 3.8 %shard_map.78 = (bf16[8,384,512]{2,1,0:T(8,128)(2,1)}, bf16[2,8,384,512]{3,2,1,0:T(8,128)(2,1)}) custom-call(bf16[8,384,512]{2,1,0:T(8,128)(2,1)S(1)} %get-tuple-element.5.traction, bf16[8,384,512]{2,1,0:T(8,128)(2,1)S(1)} %get-tuple-element.6.newest, bf16[1,8,384,512]{3,2,1,0:T(8,128)(2,1)S(1)} %get-tuple-element.7.older), custom_call_target="tpu_custom_call" | custom-call | bytes 16777216 | tf_op jit(solution)/shard_map/pallas_call | solution.py:327

commit v5 on v3

--- a/solution.py
+++ b/solution.py
@@ -93,7 +93,7 @@
     pl.semaphore_wait(barrier, jnp.where(at_end, 3, 4))
 
     def is_early(c):
-        return (c < 2 * (lag + 2)) | ~left_half
+        return (c < 2 * lag + 5) | ~left_half
 
     for c in range(here):
         @pl.when((lag < n_lag - 1) & is_early(c))
@@ -329,9 +329,10 @@
             jax.ShapeDtypeStruct((here, vec, width), kind),
             jax.ShapeDtypeStruct((lags, here, vec, width), kind),
         ),
-        in_specs=[anywhere] * 3,
+        in_specs=[pl.BlockSpec(memory_space=pltpu.VMEM)] * 3,
         out_specs=(anywhere, anywhere),
         scratch_shapes=[dma((lags + 1, here))],
+        compiler_params=pltpu.CompilerParams(vmem_limit_bytes=32 * 2**20),
         cost_estimate=pl.CostEstimate(flops=0, bytes_accessed=16 * 2**20, transcendentals=0),
     )(traction, newest, older)
 

time: 436 us -> 156 us (0.36)
  Pallas kernels: 430 us -> 155 us
  local copies, waits for them, and re-layouts: 5 us -> 0 us
    pallas_call x1, Pallas kernels: 287 us -> 3.8 us  [shards(): pl.pallas_call(place, out_shape=(jax.ShapeDtypeStruct((here, vec, width),...]
    pallas_call x1, Pallas kernels: 143 us -> 152 us  [shards(): pl.pallas_call(functools.partial(march, n_tile, n_lag), out_shape=(pltpu....]
    unnamed x6 -> x0, local copies, waits for them, and re-layouts: 5 us -> none
where the time goes in v5:
time: 156 us
  Pallas kernels  155 us (99%)
    pallas_call x1, Pallas kernels, shards(): pl.pallas_call(functools.partial(march, n_tile, n_lag), out_shape=(pltpu....  152 us
    pallas_call x1, Pallas kernels, shards(): pl.pallas_call(place, out_shape=(jax.ShapeDtypeStruct((here, vec, width),...  3.8 us

profile of v5, /device:TPU:0, one launch (start us, length us, event | category | flops | bytes accessed | tf_op | source)
XLA Modules:
  0.0 156.0 jit_solution(8891087913354448816)
XLA Ops:
  0.6 151.6 %shard_map.77 = (bf16[8,384,512]{2,1,0:T(8,128)(2,1)S(1)}, bf16[8,384,512]{2,1,0:T(8,128)(2,1)S(1)}, bf16[1,8,384,512]{3,2,1,0:T(8,128)(2,1)S(1)}) custom-call(bf16[2,8,384,512]{3,2,1,0:T(8,128)(2,1)} %history.1, bf16[2,8,2,384,384]{4,3,2,1,0:T(8,128)(2,1)} %lag_blocks.1, bf16[8,384,384]{2,1,0:T(8,128)(2,1)} %self_inverse.1, f32[8,384,512]{2,1,0:T(8,128)} %excitation.1, ...), custom_call_target="tpu_custom_call" | custom-call | flops 6039797760 | bytes 41943040 | tf_op jit(solution)/shard_map/pallas_call | solution.py:297
  152.2 3.8 %shard_map.78 = (bf16[8,384,512]{2,1,0:T(8,128)(2,1)}, bf16[2,8,384,512]{3,2,1,0:T(8,128)(2,1)}) custom-call(bf16[8,384,512]{2,1,0:T(8,128)(2,1)S(1)} %get-tuple-element.5.traction, bf16[8,384,512]{2,1,0:T(8,128)(2,1)S(1)} %get-tuple-element.6.newest, bf16[1,8,384,512]{3,2,1,0:T(8,128)(2,1)S(1)} %get-tuple-element.7.older), custom_call_target="tpu_custom_call" | custom-call | bytes 16777216 | tf_op jit(solution)/shard_map/pallas_call | solution.py:326
